TPU v7x, 512 devices: a whole 4x4x16 slice. The times are simulated.
512 devices in a mesh: row: 128 (over x, z, y_hi), ch: 4 (over y_lo, core).
Axes of the slice: x: 4, y: 4 (y_hi: 2, y_lo: 2; y = y_hi * 2 + y_lo), z: 16, core: 2. Of those that a mesh axis runs over, the one named last changes fastest.
Arguments:
- pair_rep: bfloat16 [128, 128, 128], P('ch', 'row'), may hold values from -6 to 6
- residue_mask: int32 [128], replicated, may hold values 0 or 1
- chain_ids: int32 [128], replicated, may hold values from 0 to 3, never falling along the last dimension, each value on 1 to 64 neighbouring positions
- in_gain: float32 [2, 128], replicated, may hold values from 0.5 to 1.5
- in_bias: float32 [2, 128], replicated, may hold values from -3 to 3
- w_proj: bfloat16 [2, 128, 4, 128], P(None, None, None, 'ch'), may hold values from -0.5 to 0.5
- w_gate: bfloat16 [2, 128, 128], P(None, None, 'ch'), may hold values from -0.5 to 0.5
- pair_bias: float32 [2, 128], P(None, 'ch'), may hold values from -4 to 4
- out_gain: float32 [2, 128], P(None, 'ch'), may hold values from 0.5 to 1.5
- out_bias: float32 [2, 128], P(None, 'ch'), may hold values from -3 to 3
- w_out: bfloat16 [2, 128, 128], P(None, 'ch'), may hold values from -0.5 to 0.5
Outputs:
- pair_out: bfloat16 [128, 128, 128], P('ch', 'row')
Inputs may be any that keep to these rules, and one draw needn't show every extreme that they name: `chain_ids`: chain numbers never fall along the residues; each chain has 1 to 64 residues.
All inputs are finite; a program needn't handle non-finite values.
Results may differ from a plain program's by a relative error of at most 0.013.
Values may be sent and summed in bfloat16 or wider, within the bound.
No kernel may reach another device: no remote copies, remote signals or barrier semaphores. Data moves between devices by JAX's collectives and lax.ppermute only.
A program may use at most 64 MiB of HBM per device.

v0:
```python
import jax
import jax.numpy as jnp
from jax import lax
from jax.sharding import Mesh, PartitionSpec as P

epsilon = 1e-05
bf16 = jnp.bfloat16
f32 = jnp.float32
ROW = ("x", "z", "yh")
PLANE = ("x", "yh", "ch")


def norm(v, gain, bias):
    mean = jnp.mean(v, axis=0)
    var = jnp.mean(v * v, axis=0) - mean * mean
    return ((v - mean) * lax.rsqrt(var + epsilon) * gain[:, None] + bias[:, None]).astype(bf16)


def body(
    pair_rep,
    residue_mask,
    chain_ids,
    in_gain,
    in_bias,
    w_proj,
    w_gate,
    pair_bias,
    out_gain,
    out_bias,
    w_out,
):
    ix, iz, iyh, q = (lax.axis_index(a) for a in ("x", "z", "yh", "ch"))
    row = (ix * 16 + iz) * 2 + iyh
    me = ix * 8 + iyh * 4 + q
    zfull = lax.all_gather(pair_rep[:, 0, :], "ch", axis=0, tiled=True)
    zfull, residue_mask, chain_ids, in_gain, in_bias = lax.optimization_barrier(
        (zfull, residue_mask, chain_ids, in_gain, in_bias)
    )
    mask = residue_mask.astype(f32)
    n0 = norm(zfull.astype(f32), in_gain[0], in_bias[0])
    p0 = jnp.einsum("ck,cpd->pdk", n0, w_proj[0], preferred_element_type=f32)
    pm = mask[row] * mask
    left = (jax.nn.sigmoid(p0[0]) * p0[1] * pm).astype(bf16).reshape(8, 4, 128)
    right = (jax.nn.sigmoid(p0[2]) * p0[3] * pm).astype(bf16).reshape(8, 4, 128)
    zt = lax.dynamic_index_in_dim(zfull.T.reshape(4, 8, 4, 128), q, 2, keepdims=False)
    zt = zt.transpose(1, 0, 2)
    send = jnp.stack([left, right, zt], axis=1).reshape(4, 1, 2, 3, 4, 128)
    send = jnp.broadcast_to(send, (4, 16, 2, 3, 4, 128)).reshape(128, 3, 4, 128)
    got = lax.all_to_all(send, ROW, 0, 0, tiled=True)
    w_gate2 = w_gate.transpose(1, 0, 2).reshape(2, 64, 64).transpose(1, 0, 2).reshape(64, 128)
    packed = jnp.concatenate([w_proj[1].reshape(128, 128), w_gate2, w_out.reshape(64, 128)], axis=0)
    packed = lax.all_gather(packed, "ch", axis=0)
    small = lax.all_gather(jnp.concatenate([pair_bias, out_gain, out_bias], axis=0), "ch", axis=0)
    wp1 = packed[:, :128].reshape(4, 128, 4, 32).transpose(1, 2, 0, 3).reshape(128, 4, 128)
    wg = packed[:, 128:192].reshape(4, 64, 2, 2, 32).transpose(3, 2, 1, 0, 4).reshape(2, 128, 128)
    wo = packed[:, 192:].reshape(4, 2, 32, 128)
    pbias = small[:, 0:2].transpose(1, 0, 2).reshape(2, 128)
    og, ob = (small[:, 2:4], small[:, 4:6])
    x0 = jnp.einsum("jdk,idk->dji", got[:, 1], got[:, 0], preferred_element_type=f32).astype(bf16)
    x0 = x0.reshape(4, 4, 32, 128).transpose(2, 0, 1, 3).reshape(32, 4, 512)
    x0 = lax.all_to_all(x0, PLANE, 0, 0, tiled=True).reshape(128, 512).astype(f32)

    def reorder(w):
        return w.reshape(4, 8, 4, *w.shape[2:]).swapaxes(0, 1).reshape(128, *w.shape[2:])

    cols = jnp.arange(4) * 32 + me
    same = (chain_ids[cols][:, None] == chain_ids[None, :]).astype(f32).reshape(512)
    pm1 = (mask[cols][:, None] * mask[None, :]).reshape(512)
    xn = norm(x0, reorder(og[:, 0]), reorder(ob[:, 0]))
    y = jnp.einsum("dp,dc->cp", xn, reorder(wo[:, 0]), preferred_element_type=f32)
    zp = got[:, 2].transpose(2, 1, 0).reshape(128, 512).astype(f32)
    nz = norm(zp, in_gain[0], in_bias[0])
    gate = jax.nn.sigmoid(
        jnp.einsum("cp,cd->dp", nz, wg[0], preferred_element_type=f32) + pbias[0][:, None] * same
    )
    z1 = (zp + gate * y).astype(bf16)
    n1 = norm(z1.astype(f32), in_gain[1], in_bias[1])
    p1 = jnp.einsum("cp,cxd->xdp", n1, wp1, preferred_element_type=f32)
    left1 = (jax.nn.sigmoid(p1[0]) * p1[1] * pm1).astype(bf16)
    right1 = (jax.nn.sigmoid(p1[2]) * p1[3] * pm1).astype(bf16)
    gate1 = jax.nn.sigmoid(
        jnp.einsum("cp,cd->dp", n1, wg[1], preferred_element_type=f32) + pbias[1][:, None] * same
    ).astype(bf16)
    zg = jnp.stack([z1, gate1]).reshape(2, 4, 32, 4, 4, 16, 2)
    zg = lax.dynamic_index_in_dim(zg, iz, 5, keepdims=False)
    zg = zg.transpose(4, 5, 1, 0, 3, 2).reshape(32, 4, 64)
    send = jnp.concatenate(
        [left1.reshape(32, 4, 512), right1.reshape(32, 4, 512), zg, jnp.zeros((32, 4, 64), bf16)],
        axis=2,
    )
    got = lax.all_to_all(send, PLANE, 0, 0, tiled=True)
    l1 = lax.dynamic_slice_in_dim(got[:, :, :512], iz * 2, 2, 0).reshape(2, 4, 4, 128)
    r1 = got[:, :, 512:1024].reshape(32, 4, 4, 128)
    x1 = jnp.einsum("ydxk,mdtk->xydtm", l1, r1, preferred_element_type=f32).astype(bf16)
    x1 = jnp.broadcast_to(x1.reshape(8, 1, 4, 128), (8, 4, 4, 128)).reshape(32, 4, 128)
    x1 = lax.all_to_all(x1, PLANE, 0, 0, tiled=True).reshape(128, 128).astype(f32)
    xn = norm(x1, og[:, 1].reshape(128), ob[:, 1].reshape(128))
    wo1 = lax.dynamic_slice_in_dim(wo[:, 1].reshape(128, 128), q * 32, 32, 1)
    y = jnp.einsum("dp,dc->cp", xn, wo1, preferred_element_type=f32)
    zg = (
        got[:, :, 1024:1088]
        .reshape(32, 2, 4, 32)
        .transpose(1, 3, 2, 0)
        .reshape(2, 32, 128)
        .astype(f32)
    )
    return (zg[0] + zg[1] * y).astype(bf16)[:, None, :]


def solution(mesh):
    fine = Mesh(mesh.devices.reshape(4, 16, 2, 4), ("x", "z", "yh", "ch"))
    return jax.shard_map(
        body,
        mesh=fine,
        in_specs=(
            P("ch", ROW, None),
            P(),
            P(),
            P(),
            P(),
            P(None, None, None, "ch"),
            P(None, None, "ch"),
            P(None, "ch"),
            P(None, "ch"),
            P(None, "ch"),
            P(None, "ch", None),
        ),
        out_specs=P("ch", ROW, None),
        check_vma=False,
    )
```

profile of v0, /device:TPU:1, one launch (start us, length us, event | category | flops | bytes accessed | tf_op | source)
XLA Modules:
  0.0 107.9 jit_solution(16931430102296169060)
XLA Ops:
  0.0 0.7 copy-done.4
  0.7 11.9 %all-gather.1 = bf16[128,1,128]{2,0,1:T(8,128)(2,1)S(1)} all-gather(bf16[32,1,128]{2,0,1:T(8,128)(2,1)S(1)} %copy-done.4), channel_id=3, replica_groups=mesh['x'=4,'z'=16,'yh'=2,'ch'=4] {'ch'}, dimensions={0}, use_global_device_ids=true | all-gather | bytes 40960 | tf_op jit(solution)/shard_map/all_gather | solution.py:35
  12.7 0.7 copy-done.10
  13.9 0.6 broadcast_multiply_fusion.3
  14.8 0.6 copy-done.8
  15.8 0.8 broadcast_in_dim.13
  16.7 16.9 %all-to-all-start = ((bf16[128,3,4,128]{3,2,1,0:T(4,128)(2,1)}), bf16[128,3,4,128]{3,2,1,0:T(4,128)(2,1)S(1)}, u32[]{:S(2)}, u32[]{:S(2)}) async-start(bf16[128,3,4,128]{3,2,1,0:T(4,128)(2,1)} %bitcast.25), calls=%async_computation | async-start | bytes 786432 | tf_op jit(solution)/shard_map/all_to_all | solution.py:49
  33.6 0.7 copy-done.5
  34.3 5.4 %all-gather.3 = f32[4,6,32]{2,1,0:T(8,128)S(1)} all-gather(f32[1,6,32]{2,1,0:T(8,128)S(1)} %maximum_bitcast_fusion.1), channel_id=4, replica_groups=mesh['x'=4,'z'=16,'yh'=2,'ch'=4] {'ch'}, dimensions={0}, use_global_device_ids=true | all-gather | bytes 3840 | tf_op jit(solution)/shard_map/all_gather | solution.py:53
  40.0 0.6 gather_fusion.1
  40.6 0.6 gather_fusion
  41.4 0.7 copy-done.3
  42.3 6.4 %all-gather = bf16[1024,128]{0,1:T(8,128)(2,1)S(1)} all-gather(bf16[256,128]{0,1:T(8,128)(2,1)S(1)} %pad_maximum_fusion), channel_id=2, replica_groups=mesh['x'=4,'z'=16,'yh'=2,'ch'=4] {'ch'}, dimensions={0}, use_global_device_ids=true | all-gather | bytes 327680 | tf_op jit(solution)/shard_map/all_gather | solution.py:52
  50.0 10.7 %all-to-all-done = bf16[128,3,4,128]{3,2,1,0:T(4,128)(2,1)S(1)} async-done(((bf16[128,3,4,128]{3,2,1,0:T(4,128)(2,1)}), bf16[128,3,4,128]{3,2,1,0:T(4,128)(2,1)S(1)}, u32[]{:S(2)}, u32[]{:S(2)}) %all-to-all-start) | async-done | bytes 393248 | tf_op jit(solution)/shard_map/all_to_all | solution.py:49
  61.4 0.7 copy.257
  62.2 7.9 %all-to-all-start.1 = ((bf16[32,4,512]{2,1,0:T(4,128)(2,1)}), bf16[32,4,512]{2,1,0:T(4,128)(2,1)S(1)}, u32[]{:S(2)}, u32[]{:S(2)}) async-start(bf16[32,4,512]{2,1,0:T(4,128)(2,1)} %copy.257), calls=%async_computation.1 | async-start | bytes 262144 | tf_op jit(solution)/shard_map/all_to_all | solution.py:61
  70.6 7.1 %all-to-all-done.1 = bf16[32,4,512]{2,1,0:T(4,128)(2,1)S(1)} async-done(((bf16[32,4,512]{2,1,0:T(4,128)(2,1)}), bf16[32,4,512]{2,1,0:T(4,128)(2,1)S(1)}, u32[]{:S(2)}, u32[]{:S(2)}) %all-to-all-start.1) | async-done | bytes 131104 | tf_op jit(solution)/shard_map/all_to_all | solution.py:61
  80.4 1.0 concatenate.13
  81.4 3.9 %all-to-all-start.2 = ((bf16[32,4,1152]{2,1,0:T(4,128)(2,1)}), bf16[32,4,1152]{2,1,0:T(4,128)(2,1)S(1)}, u32[]{:S(2)}, u32[]{:S(2)}) async-start(bf16[32,4,1152]{2,1,0:T(4,128)(2,1)} %concatenate.13), calls=%async_computation.2 | async-start | bytes 589824 | tf_op jit(solution)/shard_map/all_to_all | solution.py:91
  85.5 9.3 %all-to-all-done.2 = bf16[32,4,1152]{2,1,0:T(4,128)(2,1)S(1)} async-done(((bf16[32,4,1152]{2,1,0:T(4,128)(2,1)}), bf16[32,4,1152]{2,1,0:T(4,128)(2,1)S(1)}, u32[]{:S(2)}, u32[]{:S(2)}) %all-to-all-start.2) | async-done | bytes 294944 | tf_op jit(solution)/shard_map/all_to_all | solution.py:91
  95.3 0.6 broadcast_in_dim.16
  95.9 3.6 %all-to-all-start.3 = ((bf16[32,4,128]{2,1,0:T(4,128)(2,1)}), bf16[32,4,128]{2,1,0:T(4,128)(2,1)S(1)}, u32[]{:S(2)}, u32[]{:S(2)}) async-start(bf16[32,4,128]{2,1,0:T(4,128)(2,1)} %bitcast.62), calls=%async_computation.3 | async-start | bytes 65536 | tf_op jit(solution)/shard_map/all_to_all | solution.py:96
  100.1 6.8 %all-to-all-done.3 = bf16[32,4,128]{2,1,0:T(4,128)(2,1)S(1)} async-done(((bf16[32,4,128]{2,1,0:T(4,128)(2,1)}), bf16[32,4,128]{2,1,0:T(4,128)(2,1)S(1)}, u32[]{:S(2)}, u32[]{:S(2)}) %all-to-all-start.3) | async-done | bytes 32800 | tf_op jit(solution)/shard_map/all_to_all | solution.py:96
  107.0 0.9 fusion.14
  (111 shorter events, 8.1 us)
Async XLA Ops:
  0.0 0.7 copy-start.4
  12.6 2.1 %copy-start.1 = (bf16[2,128,4,32]{1,3,2,0:T(8,128)(2,1)S(1)}, bf16[2,128,4,32]{1,3,2,0:T(8,128)(2,1)}, u32[]{:S(2)}) copy-start(bf16[2,128,4,32]{1,3,2,0:T(8,128)(2,1)} %param.16) | copy-start | bytes 196612
  12.7 0.7 copy-start.10
  14.7 0.7 copy-start.8
  14.7 0.7 copy-start.9
  16.7 16.9 %copy-start.6 = (f32[2,32]{1,0:T(2,128)S(1)}, f32[2,32]{1,0:T(2,128)}, u32[]{:S(2)}) copy-start(f32[2,32]{1,0:T(2,128)} %param.19) | copy-start | bytes 772
  16.7 16.9 %copy-start.7 = (f32[2,32]{1,0:T(2,128)S(1)}, f32[2,32]{1,0:T(2,128)}, u32[]{:S(2)}) copy-start(f32[2,32]{1,0:T(2,128)} %param.18) | copy-start | bytes 772
  16.7 44.0 %all-to-all-start = ((bf16[128,3,4,128]{3,2,1,0:T(4,128)(2,1)}), bf16[128,3,4,128]{3,2,1,0:T(4,128)(2,1)S(1)}, u32[]{:S(2)}, u32[]{:S(2)}) async-start(bf16[128,3,4,128]{3,2,1,0:T(4,128)(2,1)} %bitcast.25), calls=%async_computation | async-start | bytes 786432 | tf_op jit(solution)/shard_map/all_to_all | solution.py:49
  33.6 0.7 copy-start.5
  39.9 0.7 copy-start
  40.6 0.7 copy-start.2
  41.4 0.7 copy-start.3
  62.2 15.6 %all-to-all-start.1 = ((bf16[32,4,512]{2,1,0:T(4,128)(2,1)}), bf16[32,4,512]{2,1,0:T(4,128)(2,1)S(1)}, u32[]{:S(2)}, u32[]{:S(2)}) async-start(bf16[32,4,512]{2,1,0:T(4,128)(2,1)} %copy.257), calls=%async_computation.1 | async-start | bytes 262144 | tf_op jit(solution)/shard_map/all_to_all | solution.py:61
  81.4 13.4 %all-to-all-start.2 = ((bf16[32,4,1152]{2,1,0:T(4,128)(2,1)}), bf16[32,4,1152]{2,1,0:T(4,128)(2,1)S(1)}, u32[]{:S(2)}, u32[]{:S(2)}) async-start(bf16[32,4,1152]{2,1,0:T(4,128)(2,1)} %concatenate.13), calls=%async_computation.2 | async-start | bytes 589824 | tf_op jit(solution)/shard_map/all_to_all | solution.py:91
  95.9 11.0 %all-to-all-start.3 = ((bf16[32,4,128]{2,1,0:T(4,128)(2,1)}), bf16[32,4,128]{2,1,0:T(4,128)(2,1)S(1)}, u32[]{:S(2)}, u32[]{:S(2)}) async-start(bf16[32,4,128]{2,1,0:T(4,128)(2,1)} %bitcast.62), calls=%async_computation.3 | async-start | bytes 65536 | tf_op jit(solution)/shard_map/all_to_all | solution.py:96
where the time goes:
time: 109 us; the launch traced here: 108 us
  waiting for transfers between devices  33.9 us (31%)
  starting transfers between devices  32.3 us (30%)
  blocking collectives  23.7 us (22%)
  local copies, waits for them, and re-layouts  12.5 us (11%)
  matrix products  2.7 us (2%)
  other arithmetic  2.21 us (2%)
    all_to_all x1, starting transfers between devices, body(): got = lax.all_to_all(send, ROW, 0, 0, tiled=True)  16.9 us
    all_gather x1, blocking collectives, body(): zfull = lax.all_gather(pair_rep[:, 0, :], 'ch', axis=0, tiled=True)  11.9 us
    all_to_all x1, waiting for transfers between devices, body(): got = lax.all_to_all(send, ROW, 0, 0, tiled=True)  10.7 us
    all_to_all x1, waiting for transfers between devices, body(): got = lax.all_to_all(send, PLANE, 0, 0, tiled=True)  9.26 us
    all_to_all x1, starting transfers between devices, body(): lax.all_to_all(x0, PLANE, 0, 0, tiled=True).reshape(128, 512).astype(f32)  7.85 us
    all_to_all x1, waiting for transfers between devices, body(): lax.all_to_all(x0, PLANE, 0, 0, tiled=True).reshape(128, 512).astype(f32)  7.1 us
    all_to_all x1, waiting for transfers between devices, body(): lax.all_to_all(x1, PLANE, 0, 0, tiled=True).reshape(128, 128).astype(f32)  6.79 us
    all_gather x1, blocking collectives, body(): packed = lax.all_gather(packed, 'ch', axis=0)  6.42 us
  transfers between devices with their start and end apart: 4, of which 4 were waited for; matrix products, arithmetic and copies ran while one was open for 4% of the time, Pallas kernels for 0%

commit v1 on v0

--- a/solution.py
+++ b/solution.py
@@ -32,7 +32,9 @@
     ix, iz, iyh, q = (lax.axis_index(a) for a in ("x", "z", "yh", "ch"))
     row = (ix * 16 + iz) * 2 + iyh
     me = ix * 8 + iyh * 4 + q
-    zfull = lax.all_gather(pair_rep[:, 0, :], "ch", axis=0, tiled=True)
+    zfull = jnp.concatenate(
+        lax.all_to_all(jnp.stack([pair_rep[:, 0, :]] * lax.axis_size("ch")), "ch", 0, 0), axis=0
+    )
     zfull, residue_mask, chain_ids, in_gain, in_bias = lax.optimization_barrier(
         (zfull, residue_mask, chain_ids, in_gain, in_bias)
     )

time: 109 us -> 121 us (1.11)
  waiting for transfers between devices: 33.9 us -> 47.7 us
  blocking collectives: 23.7 us -> 11.3 us
  starting transfers between devices: 32.3 us -> 42.4 us
  local copies, waits for them, and re-layouts: 12.5 us -> 13.8 us
    all_to_all x1, waiting for transfers between devices: 10.7 us -> 24.5 us  [body(): got = lax.all_to_all(send, ROW, 0, 0, tiled=True)]
    all_gather x1 -> x0, blocking collectives: 11.9 us -> none  [body(): zfull = lax.all_gather(pair_rep[:, 0, :], 'ch', axis=0, tiled=True)]
    all_to_all x0 -> x1, starting transfers between devices: none -> 10.1 us  [body(): lax.all_to_all(jnp.stack([pair_rep[:, 0, :]] * lax.axis_size('ch')), 'ch'...]
    another operation x0 -> x1, local copies, waits for them, and re-layouts: none -> 1.33 us  [body(): jnp.stack([pair_rep[:, 0, :]] * lax.axis_size('ch'))]
    unnamed x23 -> x21, local copies, waits for them, and re-layouts: 3.48 us -> 3.42 us
  transfers between devices with their start and end apart: 4 -> 5, of which waited for: 4 -> 4; matrix products, arithmetic and copies ran while one was open for 4% -> 3% of each run, Pallas kernels for 0% -> 0%
where the time goes in v1:
time: 121 us; the launch traced here: 120 us
  waiting for transfers between devices  47.7 us (39%)
  starting transfers between devices  42.4 us (35%)
  local copies, waits for them, and re-layouts  13.8 us (11%)
  blocking collectives  11.3 us (9%)
  matrix products  2.7 us (2%)
  other arithmetic  2.13 us (2%)
    all_to_all x1, waiting for transfers between devices, body(): got = lax.all_to_all(send, ROW, 0, 0, tiled=True)  24.5 us
    all_to_all x1, starting transfers between devices, body(): got = lax.all_to_all(send, ROW, 0, 0, tiled=True)  16.8 us
    all_to_all x1, starting transfers between devices, body(): lax.all_to_all(jnp.stack([pair_rep[:, 0, :]] * lax.axis_size('ch')), 'ch'...  10.1 us
    all_to_all x1, waiting for transfers between devices, body(): got = lax.all_to_all(send, PLANE, 0, 0, tiled=True)  9.26 us
    all_to_all x1, starting transfers between devices, body(): lax.all_to_all(x0, PLANE, 0, 0, tiled=True).reshape(128, 512).astype(f32)  8 us
    all_to_all x1, waiting for transfers between devices, body(): lax.all_to_all(x0, PLANE, 0, 0, tiled=True).reshape(128, 512).astype(f32)  7.1 us
    all_to_all x1, waiting for transfers between devices, body(): lax.all_to_all(x1, PLANE, 0, 0, tiled=True).reshape(128, 128).astype(f32)  6.79 us
    all_gather x1, blocking collectives, body(): packed = lax.all_gather(packed, 'ch', axis=0)  6.12 us
  transfers between devices with their start and end apart: 5, of which 4 were waited for; matrix products, arithmetic and copies ran while one was open for 3% of the time, Pallas kernels for 0%

profile of v1, /device:TPU:1, one launch (start us, length us, event | category | flops | bytes accessed | tf_op | source)
XLA Modules:
  0.0 120.5 jit_solution(11215278988244412929)
XLA Ops:
  0.0 1.3 %stack.18 = bf16[4,32,128]{2,1,0:T(8,128)(2,1)} broadcast(bf16[32,128]{1,0:T(8,128)(2,1)} %bitcast.174), dimensions={1,2} | broadcast | bytes 40960 | tf_op jit(solution)/shard_map/stack | solution.py:36
  1.3 10.1 %all-to-all-start = ((bf16[4,32,128]{2,1,0:T(8,128)(2,1)}), bf16[4,32,128]{2,1,0:T(8,128)(2,1)S(1)}, u32[]{:S(2)}, u32[]{:S(2)}) async-start(bf16[4,32,128]{2,1,0:T(8,128)(2,1)} %stack.18), calls=%async_computation | async-start | bytes 65536 | tf_op jit(solution)/shard_map/all_to_all | solution.py:36
  11.5 0.7 copy-done.2
  12.3 0.7 copy-done.3
  13.2 6.1 %all-gather = bf16[1024,128]{0,1:T(8,128)(2,1)S(1)} all-gather(bf16[256,128]{0,1:T(8,128)(2,1)S(1)} %pad_maximum_fusion), channel_id=2, replica_groups=mesh['x'=4,'z'=16,'yh'=2,'ch'=4] {'ch'}, dimensions={0}, use_global_device_ids=true | all-gather | bytes 327680 | tf_op jit(solution)/shard_map/all_gather | solution.py:54
  19.5 0.6 copy-done.4
  20.2 5.1 %all-gather.2 = f32[4,6,32]{2,1,0:T(8,128)S(1)} all-gather(f32[1,6,32]{2,1,0:T(8,128)S(1)} %maximum_bitcast_fusion.1), channel_id=3, replica_groups=mesh['x'=4,'z'=16,'yh'=2,'ch'=4] {'ch'}, dimensions={0}, use_global_device_ids=true | all-gather | bytes 3840 | tf_op jit(solution)/shard_map/all_gather | solution.py:55
  25.4 0.7 copy-done.9
  26.6 0.6 broadcast_multiply_fusion.3
  27.4 0.6 copy-done.7
  28.5 0.8 broadcast_in_dim.13
  29.4 16.8 %all-to-all-start.1 = ((bf16[128,3,4,128]{3,2,1,0:T(4,128)(2,1)}), bf16[128,3,4,128]{3,2,1,0:T(4,128)(2,1)S(1)}, u32[]{:S(2)}, u32[]{:S(2)}) async-start(bf16[128,3,4,128]{3,2,1,0:T(4,128)(2,1)} %bitcast.26), calls=%async_computation.1 | async-start | bytes 786432 | tf_op jit(solution)/shard_map/all_to_all | solution.py:51
  47.2 0.6 gather_fusion.1
  47.9 0.6 gather_fusion
  48.7 24.5 %all-to-all-done.1 = bf16[128,3,4,128]{3,2,1,0:T(4,128)(2,1)S(1)} async-done(((bf16[128,3,4,128]{3,2,1,0:T(4,128)(2,1)}), bf16[128,3,4,128]{3,2,1,0:T(4,128)(2,1)S(1)}, u32[]{:S(2)}, u32[]{:S(2)}) %all-to-all-start.1) | async-done | bytes 393248 | tf_op jit(solution)/shard_map/all_to_all | solution.py:51
  73.9 0.7 copy.250
  74.7 8.0 %all-to-all-start.2 = ((bf16[32,4,512]{2,1,0:T(4,128)(2,1)}), bf16[32,4,512]{2,1,0:T(4,128)(2,1)S(1)}, u32[]{:S(2)}, u32[]{:S(2)}) async-start(bf16[32,4,512]{2,1,0:T(4,128)(2,1)} %copy.250), calls=%async_computation.2 | async-start | bytes 262144 | tf_op jit(solution)/shard_map/all_to_all | solution.py:63
  83.3 7.1 %all-to-all-done.2 = bf16[32,4,512]{2,1,0:T(4,128)(2,1)S(1)} async-done(((bf16[32,4,512]{2,1,0:T(4,128)(2,1)}), bf16[32,4,512]{2,1,0:T(4,128)(2,1)S(1)}, u32[]{:S(2)}, u32[]{:S(2)}) %all-to-all-start.2) | async-done | bytes 131104 | tf_op jit(solution)/shard_map/all_to_all | solution.py:63
  93.0 1.0 concatenate.13
  94.0 3.9 %all-to-all-start.3 = ((bf16[32,4,1152]{2,1,0:T(4,128)(2,1)}), bf16[32,4,1152]{2,1,0:T(4,128)(2,1)S(1)}, u32[]{:S(2)}, u32[]{:S(2)}) async-start(bf16[32,4,1152]{2,1,0:T(4,128)(2,1)} %concatenate.13), calls=%async_computation.3 | async-start | bytes 589824 | tf_op jit(solution)/shard_map/all_to_all | solution.py:93
  98.1 9.3 %all-to-all-done.3 = bf16[32,4,1152]{2,1,0:T(4,128)(2,1)S(1)} async-done(((bf16[32,4,1152]{2,1,0:T(4,128)(2,1)}), bf16[32,4,1152]{2,1,0:T(4,128)(2,1)S(1)}, u32[]{:S(2)}, u32[]{:S(2)}) %all-to-all-start.3) | async-done | bytes 294944 | tf_op jit(solution)/shard_map/all_to_all | solution.py:93
  108.6 3.6 %all-to-all-start.4 = ((bf16[32,4,128]{2,1,0:T(4,128)(2,1)}), bf16[32,4,128]{2,1,0:T(4,128)(2,1)S(1)}, u32[]{:S(2)}, u32[]{:S(2)}) async-start(bf16[32,4,128]{2,1,0:T(4,128)(2,1)} %bitcast.63), calls=%async_computation.4 | async-start | bytes 65536 | tf_op jit(solution)/shard_map/all_to_all | solution.py:98
  112.8 6.8 %all-to-all-done.4 = bf16[32,4,128]{2,1,0:T(4,128)(2,1)S(1)} async-done(((bf16[32,4,128]{2,1,0:T(4,128)(2,1)}), bf16[32,4,128]{2,1,0:T(4,128)(2,1)S(1)}, u32[]{:S(2)}, u32[]{:S(2)}) %all-to-all-start.4) | async-done | bytes 32800 | tf_op jit(solution)/shard_map/all_to_all | solution.py:98
  119.6 0.9 fusion.14
  (111 shorter events, 8.6 us)
Async XLA Ops:
  0.0 11.4 %copy-start.1 = (bf16[2,128,4,32]{1,3,2,0:T(8,128)(2,1)S(1)}, bf16[2,128,4,32]{1,3,2,0:T(8,128)(2,1)}, u32[]{:S(2)}) copy-start(bf16[2,128,4,32]{1,3,2,0:T(8,128)(2,1)} %param.16) | copy-start | bytes 196612
  1.3 24.1 %all-to-all-start = ((bf16[4,32,128]{2,1,0:T(8,128)(2,1)}), bf16[4,32,128]{2,1,0:T(8,128)(2,1)S(1)}, u32[]{:S(2)}, u32[]{:S(2)}) async-start(bf16[4,32,128]{2,1,0:T(8,128)(2,1)} %stack.18), calls=%async_computation | async-start | bytes 65536 | tf_op jit(solution)/shard_map/all_to_all | solution.py:36
  11.4 0.7 copy-start.2
  12.2 0.7 copy-start.3
  19.5 0.7 copy-start.4
  19.5 0.7 copy-start.5
  19.5 0.7 copy-start.6
  25.4 0.7 copy-start.9
  27.3 0.7 copy-start.7
  27.3 0.7 copy-start.8
  29.4 43.8 %all-to-all-start.1 = ((bf16[128,3,4,128]{3,2,1,0:T(4,128)(2,1)}), bf16[128,3,4,128]{3,2,1,0:T(4,128)(2,1)S(1)}, u32[]{:S(2)}, u32[]{:S(2)}) async-start(bf16[128,3,4,128]{3,2,1,0:T(4,128)(2,1)} %bitcast.26), calls=%async_computation.1 | async-start | bytes 786432 | tf_op jit(solution)/shard_map/all_to_all | solution.py:51
  47.2 0.7 copy-start
  74.7 15.7 %all-to-all-start.2 = ((bf16[32,4,512]{2,1,0:T(4,128)(2,1)}), bf16[32,4,512]{2,1,0:T(4,128)(2,1)S(1)}, u32[]{:S(2)}, u32[]{:S(2)}) async-start(bf16[32,4,512]{2,1,0:T(4,128)(2,1)} %copy.250), calls=%async_computation.2 | async-start | bytes 262144 | tf_op jit(solution)/shard_map/all_to_all | solution.py:63
  94.0 13.4 %all-to-all-start.3 = ((bf16[32,4,1152]{2,1,0:T(4,128)(2,1)}), bf16[32,4,1152]{2,1,0:T(4,128)(2,1)S(1)}, u32[]{:S(2)}, u32[]{:S(2)}) async-start(bf16[32,4,1152]{2,1,0:T(4,128)(2,1)} %concatenate.13), calls=%async_computation.3 | async-start | bytes 589824 | tf_op jit(solution)/shard_map/all_to_all | solution.py:93
  108.6 11.0 %all-to-all-start.4 = ((bf16[32,4,128]{2,1,0:T(4,128)(2,1)}), bf16[32,4,128]{2,1,0:T(4,128)(2,1)S(1)}, u32[]{:S(2)}, u32[]{:S(2)}) async-start(bf16[32,4,128]{2,1,0:T(4,128)(2,1)} %bitcast.63), calls=%async_computation.4 | async-start | bytes 65536 | tf_op jit(solution)/shard_map/all_to_all | solution.py:98
